TPU v7x, 32 devices: a whole 2x2x4 slice. The times are simulated.
32 devices in a mesh: seq: 4 (over z), exp: 8 (over y, x, core).
Axes of the slice: x: 2, y: 2, z: 4, core: 2. Of those that a mesh axis runs over, the one named last changes fastest.
Arguments:
- tokens: bfloat16 [6144, 2048], P(('seq', 'exp')), may hold values from -1500 to 1500
- norm_gain: float32 [2048], replicated, may hold values from 0.1 to 1.9
- norm_bias: float32 [2048], replicated, may hold values from -3 to 3
- routes: int32 [6144, 6], P(('seq', 'exp')), may hold values from 0 to 7, as said below
- gate_codes: int32 [6144, 6], P(('seq', 'exp')), may hold values from 1 to 1023
- w_in: bfloat16 [8, 2048, 1408], P('exp'), may hold values from -0.125 to 0.125
- w_out: bfloat16 [8, 704, 2048], P('exp'), may hold values from -0.21875 to 0.21875
Outputs:
- mixed: bfloat16 [6144, 2048], P(('seq', 'exp'))
Inputs may be any that keep to these rules, and one draw needn't show every extreme that they name: `routes`: each row names 6 different experts; in the rows of every device one and the same expert is named exactly 192 times, more often than any other; every other expert is named at most 182 times there; one expert other than it is named exactly 182 times by the rows of every device.
All inputs are finite; a program needn't handle non-finite values.
Results may differ from a plain program's by a relative error of at most 0.0071.
Values may be sent and summed in bfloat16 or wider, within the bound.
A program may use at most 128 MiB of HBM per device.

v0:
```python
import jax
import jax.numpy as jnp
from jax import lax
from jax.sharding import PartitionSpec as P


def broadcast(value, axis, source):
    kept = jnp.where(lax.axis_index(axis) == source, value, 0).astype(value.dtype)
    return lax.psum(kept, axis)


def layer_norm(tokens, norm_gain, norm_bias):
    values = tokens.astype(jnp.float32)
    average = jnp.mean(values, axis=1, keepdims=True)
    centered = values - average
    variance = jnp.mean(centered * centered, axis=1, keepdims=True)
    return (centered * lax.rsqrt(variance + 1e-05) * norm_gain + norm_bias).astype(jnp.bfloat16)


def expert_rows(inputs, weight_in, weight_out):
    inner_width = weight_out.shape[0]
    projected = jnp.dot(inputs, weight_in, preferred_element_type=jnp.float32)
    hidden = (jax.nn.silu(projected[:, :inner_width]) * projected[:, inner_width:]).astype(
        jnp.bfloat16
    )
    return jnp.dot(hidden, weight_out, preferred_element_type=jnp.float32).astype(jnp.bfloat16)


def local(tokens, norm_gain, norm_bias, routes, gate_codes, w_in, w_out):
    owners = lax.axis_size("exp")
    count_rows, features = tokens.shape
    top_slots = routes.shape[1]
    capacity = min(count_rows, count_rows * top_slots * 9 // (8 * owners))
    slot_total = owners * capacity
    normed = layer_norm(tokens, norm_gain, norm_bias)
    gate_vals = gate_codes.astype(jnp.float32) * (1.0 / 1024.0)
    flat_ids = routes.reshape(-1)
    one_hot = (flat_ids[:, None] == jnp.arange(owners, dtype=jnp.int32)[None, :]).astype(jnp.int32)
    expert_counts = jnp.sum(one_hot, axis=0)
    hot_expert = jnp.argmax(expert_counts)
    earlier = jnp.cumsum(one_hot, axis=0) - one_hot
    slot_rank = jnp.sum(earlier * one_hot, axis=1)
    kept_mask = (flat_ids != hot_expert) & (slot_rank < capacity)
    slot_index = jnp.where(kept_mask, flat_ids * capacity + slot_rank, slot_total)
    token_index = jnp.arange(count_rows * top_slots, dtype=jnp.int32) // top_slots
    slot_token = (
        jnp.full((slot_total,), count_rows, jnp.int32).at[slot_index].set(token_index, mode="drop")
    )
    padded_rows = jnp.concatenate([normed, jnp.zeros((1, features), jnp.bfloat16)], axis=0)
    outgoing = padded_rows[slot_token].reshape(owners, capacity, features)
    weight_in = w_in[0]
    weight_out = w_out[0]
    received = lax.all_to_all(outgoing, "exp", split_axis=0, concat_axis=0, tiled=True)
    served = received.shape[1]
    results = expert_rows(received.reshape(owners * served, features), weight_in, weight_out)
    returned = lax.all_to_all(
        results.reshape(owners, served, features), "exp", split_axis=0, concat_axis=0, tiled=True
    )
    groups = lax.axis_size("seq")
    share = features // groups
    start = lax.axis_index("seq") * share
    piece_in = lax.dynamic_slice_in_dim(w_in, start, share, 1)
    piece_down = lax.dynamic_slice_in_dim(w_out, start, share, 2)
    shared_in, shared_down = (
        broadcast(piece_in, "exp", hot_expert),
        broadcast(piece_down, "exp", hot_expert),
    )
    hot_in, hot_down = (
        lax.all_gather(shared_in, "seq", axis=1, tiled=True),
        lax.all_gather(shared_down, "seq", axis=2, tiled=True),
    )
    hot_rows = expert_rows(normed, hot_in[0], hot_down[0])
    padded_back = jnp.concatenate(
        [returned.reshape(slot_total, features), jnp.zeros((1, features), jnp.bfloat16)], axis=0
    )
    picked = padded_back[slot_index].reshape(count_rows, top_slots, features)
    routed_weight = jnp.where(kept_mask, gate_vals.reshape(-1), 0.0).reshape(count_rows, top_slots)
    hot_weight = jnp.sum(jnp.where(routes == hot_expert, gate_vals, 0.0), axis=1)
    routed = jnp.sum(picked.astype(jnp.float32) * routed_weight[:, :, None], axis=1)
    mixed = routed + hot_weight[:, None] * hot_rows.astype(jnp.float32)
    return mixed.astype(jnp.bfloat16)


def solution(mesh):
    return jax.shard_map(
        local,
        mesh=mesh,
        in_specs=(
            P(("seq", "exp"), None),
            P(),
            P(),
            P(("seq", "exp"), None),
            P(("seq", "exp"), None),
            P("exp", None, None),
            P("exp", None, None),
        ),
        out_specs=P(("seq", "exp"), None),
        check_vma=False,
    )
```

profile of v0, /device:TPU:0, one launch (start us, length us, event | category | flops | bytes accessed | tf_op | source)
XLA Modules:
  0.0 291.9 jit_solution(13346570410345256110)
XLA Ops:
  6.5 0.0 copy-start.2
  6.5 0.0 copy-start.5
  6.5 0.0 copy-start
  6.5 0.0 all-reduce.5.cloned.1.call-start
  6.5 0.9 copy.18
  7.4 0.1 eq.39
  7.6 0.1 eq.35
  7.7 2.3 reduce-window.6
  10.0 0.3 slice_reduce_fusion
  10.3 0.2 reduce-window.9
  10.5 0.1 add_bitcast_fusion
  10.6 0.1 fusion.36
  10.7 0.7 iota_reduce_fusion
  12.1 0.0 copy-start.3
  12.1 0.0 copy-start.4
  12.1 2.7 dynamic-slice_select_fusion
  14.8 2.1 dynamic-slice_select_fusion.1
  16.9 0.0 all-reduce.5.cloned.1.call-update
  17.0 0.0 copy-done.2
  17.0 0.2 lt.53
  17.1 0.1 copy.22
  17.2 0.0 copy-done.5
  17.2 0.7 and_select_fusion.1
  18.0 0.2 copy.19
  18.1 0.2 ne.38
  18.3 0.1 copy.21
  18.4 0.1 mul.85
  18.6 0.0 copy-done
  18.6 0.2 convert_reduce_fusion
  18.8 0.4 fusion.27
  19.2 0.0 copy-done.3
  19.2 0.0 copy-done.4
  19.2 0.4 fusion.30
  19.7 0.1 concatenate.6
  19.7 6.4 %scatter_custom_fusion = s32[1296]{0:T(1024)S(1)} fusion(s32[1152]{0:T(1024)S(1)} %get-tuple-element.10, s32[1152]{0:T(1024)S(1)} %add_select_fusion, s32[]{:T(128)} %constant.24.clone.1), kind=kCustom, calls=%fused_computation.64 | custom fusion | bytes 5188 | tf_op jit(solution)/shard_map/scatter | solution.py:47
  26.2 6.7 %gather_fusion = bf16[1296,2048]{1,0:T(8,128)(2,1)} fusion(bf16[193,2048]{1,0:T(8,128)(2,1)S(1)} %concatenate.6, s32[2048]{0:T(1024)S(1)} %pad_clamp_fusion.1), kind=kCustom, calls=%fused_computation | custom fusion | bytes 10622016 | tf_op jit(solution)/shard_map/gather | solution.py:50
  32.9 5.0 %reshape.126 = bf16[8,162,2048]{2,1,0:T(8,128)(2,1)} reshape(bf16[1296,2048]{1,0:T(8,128)(2,1)} %gather_fusion) | data formatting | bytes 10616832 | tf_op jit(solution)/shard_map/reshape | solution.py:50
  38.0 5.1 %all-to-all-start = ((bf16[8,162,2048]{2,1,0:T(8,128)(2,1)}), bf16[8,162,2048]{2,1,0:T(8,128)(2,1)}, u32[]{:S(2)}, u32[]{:S(2)}) async-start(bf16[8,162,2048]{2,1,0:T(8,128)(2,1)} %reshape.126), calls=%async_computation | async-start | bytes 11010048 | tf_op jit(solution)/shard_map/all_to_all | solution.py:53
  43.1 0.0 all-gather.3.cloned.1.call-start
  43.1 68.6 %all-reduce.5.cloned.1.call-done = (bf16[1,704,512]{2,1,0:T(8,128)(2,1)}, bf16[1,512,1408]{2,1,0:T(8,128)(2,1)}) async-done(((bf16[1,704,512]{2,1,0:T(8,128)(2,1)}, bf16[1,512,1408]{2,1,0:T(8,128)(2,1)}), (bf16[1,704,512]{2,1,0:T(8,128)(2,1)}, bf16[1,512,1408]{2,1,0:T(8,128)(2,1)})) %all-reduce.5.cloned.1.call-update) | async-done | bytes 2162704 | tf_op jit(solution)/shard_map/psum | solution.py:9
  111.8 0.0 all-gather.3.cloned.1.call-update
  111.8 8.6 %all-to-all-done = bf16[8,162,2048]{2,1,0:T(8,128)(2,1)} async-done(((bf16[8,162,2048]{2,1,0:T(8,128)(2,1)}), bf16[8,162,2048]{2,1,0:T(8,128)(2,1)}, u32[]{:S(2)}, u32[]{:S(2)}) %all-to-all-start) | async-done | bytes 5308448 | tf_op jit(solution)/shard_map/all_to_all | solution.py:53
  120.4 5.2 %reshape.127 = bf16[1296,2048]{1,0:T(8,128)(2,1)} reshape(bf16[8,162,2048]{2,1,0:T(8,128)(2,1)} %all-to-all-done) | data formatting | bytes 10616832 | tf_op jit(solution)/shard_map/reshape | solution.py:55
  125.6 0.0 copy-start.1
  125.6 12.5 %fusion.2 = f32[1296,1408]{1,0:T(8,128)S(1)} fusion(bf16[1296,2048]{1,0:T(8,128)(2,1)} %reshape.127, bf16[1,2048,1408]{2,1,0:T(8,128)(2,1)} %param.12), kind=kOutput, calls=%fused_computation.7 | convolution fusion | flops 7474249728 | bytes 18374656 | tf_op jit(solution)/shard_map/dot_general | solution.py:22
  138.1 0.0 copy-done.1
  138.1 6.3 %convolution_convert_fusion = bf16[1296,2048]{1,0:T(8,128)(2,1)} fusion(bf16[1,704,2048]{2,1,0:T(8,128)(2,1)S(1)} %copy-done.1, f32[1296,1408]{1,0:T(8,128)S(1)} %fusion.2), kind=kOutput, calls=%fused_computation.4 | convolution fusion | flops 3745253376 | bytes 16154624 | tf_op jit(solution)/shard_map/dot_general | solution.py:26
  144.4 4.9 %reshape.128 = bf16[8,162,2048]{2,1,0:T(8,128)(2,1)} reshape(bf16[1296,2048]{1,0:T(8,128)(2,1)} %convolution_convert_fusion) | data formatting | bytes 10616832 | tf_op jit(solution)/shard_map/reshape | solution.py:57
  149.3 4.7 %all-to-all-start.1 = ((bf16[8,162,2048]{2,1,0:T(8,128)(2,1)}), bf16[8,162,2048]{2,1,0:T(8,128)(2,1)}, u32[]{:S(2)}, u32[]{:S(2)}) async-start(bf16[8,162,2048]{2,1,0:T(8,128)(2,1)} %reshape.128), calls=%async_computation.1 | async-start | bytes 11010048 | tf_op jit(solution)/shard_map/all_to_all | solution.py:56
  154.0 0.2 all-gather.5.cloned.1.call-start
  154.3 0.5 all-gather.5.cloned.1.call-update
  154.8 0.1 copy.23
  154.9 62.3 %all-to-all-done.1 = bf16[8,162,2048]{2,1,0:T(8,128)(2,1)} async-done(((bf16[8,162,2048]{2,1,0:T(8,128)(2,1)}), bf16[8,162,2048]{2,1,0:T(8,128)(2,1)}, u32[]{:S(2)}, u32[]{:S(2)}) %all-to-all-start.1) | async-done | bytes 5308448 | tf_op jit(solution)/shard_map/all_to_all | solution.py:56
  217.2 4.9 %reshape.129 = bf16[1296,2048]{1,0:T(8,128)(2,1)} reshape(bf16[8,162,2048]{2,1,0:T(8,128)(2,1)} %all-to-all-done.1) | data formatting | bytes 10616832 | tf_op jit(solution)/shard_map/reshape | solution.py:74
  222.1 5.7 %concatenate.7 = bf16[1297,2048]{1,0:T(8,128)(2,1)} pad(bf16[1296,2048]{1,0:T(8,128)(2,1)} %reshape.129, bf16[]{:T(256)} %constant.18.clone.1), padding=0_1x0_0 | pad | bytes 10620930 | tf_op jit(solution)/shard_map/concatenate | solution.py:73
  227.8 14.3 %gather_fusion.1 = bf16[1152,2048]{1,0:T(8,128)(2,1)} fusion(bf16[1297,2048]{1,0:T(8,128)(2,1)} %concatenate.7, s32[2048]{0:T(1024)S(1)} %pad_clamp_fusion), kind=kCustom, calls=%fused_computation.1 | custom fusion | bytes 9441792 | tf_op jit(solution)/shard_map/gather | solution.py:76
  242.1 9.2 %reshape.130 = f32[192,6,2048]{2,1,0:T(8,128)} reshape(bf16[1152,2048]{1,0:T(8,128)(2,1)} %gather_fusion.1) | data formatting | bytes 14155776 | tf_op jit(solution)/shard_map/convert_element_type | solution.py:79
  251.2 9.6 %multiply_reduce_fusion = f32[192,2048]{1,0:T(8,128)S(1)} fusion(f32[192,6,2048]{2,1,0:T(8,128)} %reshape.130, f32[192,6]{1,0:T(8,128)S(1)} %copy.23), kind=kLoop, calls=%fused_computation.3 | loop fusion | flops 4325376 | bytes 11014656 | tf_op jit(solution)/shard_map/reduce_sum | solution.py:79
  260.8 0.0 all-gather.3.cloned.1.call-done
  260.8 5.0 %fusion = f32[192,1408]{1,0:T(8,128)} fusion(bf16[192,2048]{1,0:T(8,128)(2,1)S(1)} %fusion.30, bf16[1,2048,1408]{2,1,0:T(8,128)(2,1)} %all-gather.3.cloned.1.call-done), kind=kOutput, calls=%fused_computation.5 | convolution fusion | flops 1107296256 | bytes 7634944 | tf_op jit(solution)/shard_map/dot_general | solution.py:22
  265.9 15.6 %all-gather.5.cloned.1.call-done = bf16[1,704,2048]{2,1,0:T(8,128)(2,1)} async-done(((bf16[1,704,512]{2,1,0:T(8,128)(2,1)}), bf16[1,704,2048]{2,1,0:T(8,128)(2,1)}) %all-gather.5.cloned.1.call-update) | async-done | bytes 2883600 | tf_op jit(solution)/shard_map/all_gather | solution.py:70
  281.5 3.9 %fusion.20 = bf16[192,2048]{1,0:T(8,128)(2,1)} fusion(f32[192,2048]{1,0:T(8,128)S(1)} %multiply_reduce_fusion, bf16[1,704,2048]{2,1,0:T(8,128)(2,1)} %all-gather.5.cloned.1.call-done, f32[192]{0:T(256)S(1)} %get-tuple-element.15, f32[192,1408]{1,0:T(8,128)} %fusion), kind=kOutput, calls=%fused_computation.18 | convolution fusion | flops 556425216 | bytes 6423296 | tf_op jit(solution)/shard_map/dot_general | solution.py:26
  (10 shorter events, 0.1 us)
Async XLA Ops:
  6.5 10.4 %copy-start.2 = (s32[192,6]{0,1:T(8,128)S(1)}, s32[192,6]{0,1:T(8,128)}, u32[]{:S(2)}) copy-start(s32[192,6]{0,1:T(8,128)} %param.10) | copy-start | bytes 13828
  6.5 10.7 %copy-start.5 = (s32[192,6]{0,1:T(8,128)S(1)}, s32[192,6]{0,1:T(8,128)}, u32[]{:S(2)}) copy-start(s32[192,6]{0,1:T(8,128)} %param.11) | copy-start | bytes 13828
  6.5 12.0 %copy-start = (bf16[192,2048]{1,0:T(8,128)(2,1)S(1)}, bf16[192,2048]{1,0:T(8,128)(2,1)}, u32[]{:S(2)}) copy-start(bf16[192,2048]{1,0:T(8,128)(2,1)} %param.7) | copy-start | bytes 2359300
  6.5 105.2 %all-reduce.5.cloned.1.call-start = ((), (), s32[]{:S(2)}) async-start(), calls=%async_computation.4 | async-start | bytes 4325376 | tf_op jit(solution)/shard_map/psum | solution.py:9
  12.1 7.1 %copy-start.3 = (f32[2048]{0:T(1024)S(1)}, f32[2048]{0:T(1024)}, u32[]{:S(2)}) copy-start(f32[2048]{0:T(1024)} %param.9) | copy-start | bytes 24580
  12.1 7.1 %copy-start.4 = (f32[2048]{0:T(1024)S(1)}, f32[2048]{0:T(1024)}, u32[]{:S(2)}) copy-start(f32[2048]{0:T(1024)} %param.8) | copy-start | bytes 24580
  38.0 82.4 %all-to-all-start = ((bf16[8,162,2048]{2,1,0:T(8,128)(2,1)}), bf16[8,162,2048]{2,1,0:T(8,128)(2,1)}, u32[]{:S(2)}, u32[]{:S(2)}) async-start(bf16[8,162,2048]{2,1,0:T(8,128)(2,1)} %reshape.126), calls=%async_computation | async-start | bytes 11010048 | tf_op jit(solution)/shard_map/all_to_all | solution.py:53
  43.1 217.7 %all-gather.3.cloned.1.call-start = ((), (), s32[]{:S(2)}) async-start(), calls=%async_computation.2 | async-start | bytes 7208960 | tf_op jit(solution)/shard_map/all_gather | solution.py:69
  125.6 12.5 %copy-start.1 = (bf16[1,704,2048]{2,1,0:T(8,128)(2,1)S(1)}, bf16[1,704,2048]{2,1,0:T(8,128)(2,1)}, u32[]{:S(2)}) copy-start(bf16[1,704,2048]{2,1,0:T(8,128)(2,1)} %param.13) | copy-start | bytes 8650756
  149.3 67.9 %all-to-all-start.1 = ((bf16[8,162,2048]{2,1,0:T(8,128)(2,1)}), bf16[8,162,2048]{2,1,0:T(8,128)(2,1)}, u32[]{:S(2)}, u32[]{:S(2)}) async-start(bf16[8,162,2048]{2,1,0:T(8,128)(2,1)} %reshape.128), calls=%async_computation.1 | async-start | bytes 11010048 | tf_op jit(solution)/shard_map/all_to_all | solution.py:56
  154.0 127.4 %all-gather.5.cloned.1.call-start = ((), (), s32[]{:S(2)}) async-start(), calls=%async_computation.3 | async-start | bytes 3604480 | tf_op jit(solution)/shard_map/all_gather | solution.py:70
Sparse Core Ops, SparseCore 0:
  17.1 94.6 all-reduce.4
  113.3 109.0 all-gather.2
  224.0 57.4 all-gather.4
where the time goes:
time: 293 us; the launch traced here: 292 us
  waiting for transfers between devices  156 us (53%)
  local copies, waits for them, and re-layouts  64.9 us (22%)
  matrix products  27.7 us (9%)
  other arithmetic  19.5 us (7%)
  between operations  14.1 us (5%)
  starting transfers between devices  10.1 us (3%)
    psum x1, waiting for transfers between devices, broadcast(): return lax.psum(kept, axis)  68.6 us
    all_to_all x1, waiting for transfers between devices, local(): lax.all_to_all(results.reshape(owners, served, features), 'exp', split_ax...  62.3 us
    dot_general x2, matrix products, expert_rows(): projected = jnp.dot(inputs, weight_in, preferred_element_type=jnp.float32)  17.5 us
    all_gather x1, waiting for transfers between devices, local(): lax.all_gather(shared_down, 'seq', axis=2, tiled=True)  15.6 us
    gather x1, local copies, waits for them, and re-layouts, local(): picked = padded_back[slot_index].reshape(count_rows, top_slots, features)  14.3 us
    dot_general x2, matrix products, expert_rows(): jnp.dot(hidden, weight_out, preferred_element_type=jnp.float32)  10.2 us
    reduce_sum x1, other arithmetic, local(): jnp.sum(picked.astype(jnp.float32) * routed_weight[:, :, None], axis=1)  9.56 us
    convert_element_type x1, local copies, waits for them, and re-layouts, local(): picked.astype(jnp.float32) * routed_weight[:, :, None]  9.16 us
  transfers between devices with their start and end apart: 5, of which 4 were waited for; matrix products, arithmetic and copies ran while one was open for 34% of the time, Pallas kernels for 0%

commit v1 on v0

v1 whole, which is shorter than its diff:
```python
import jax
import jax.numpy as jnp
from jax import lax
from jax.sharding import PartitionSpec as P


def layer_norm(tokens, norm_gain, norm_bias):
    values = tokens.astype(jnp.float32)
    average = jnp.mean(values, axis=1, keepdims=True)
    centered = values - average
    variance = jnp.mean(centered * centered, axis=1, keepdims=True)
    return (centered * lax.rsqrt(variance + 1e-05) * norm_gain + norm_bias).astype(jnp.bfloat16)


def row_codes(routes, gate_codes, owners, capacity):
    rows = routes.shape[0]
    match = routes[:, :, None] == jnp.arange(owners, dtype=jnp.int32)[None, None, :]
    codes = jnp.sum(jnp.where(match, gate_codes[:, :, None], 0), axis=1).astype(jnp.float32)
    named = jnp.any(match, axis=1)
    before = lax.broadcasted_iota(jnp.int32, (rows, rows), 1) < lax.broadcasted_iota(
        jnp.int32, (rows, rows), 0
    )
    named_b = named.astype(jnp.bfloat16)
    rank = jnp.dot(before.astype(jnp.bfloat16), named_b, preferred_element_type=jnp.float32)
    hot = jnp.argmax(jnp.sum(named.astype(jnp.float32), axis=0))
    kept = (rank < capacity) | (jnp.arange(owners)[None, :] == hot)
    return jnp.where(kept, codes, 0.0)


def local(tokens, norm_gain, norm_bias, routes, gate_codes, w_in, w_out):
    owners = lax.axis_size("exp")
    rows = tokens.shape[0]
    capacity = min(rows, rows * routes.shape[1] * 9 // (8 * owners))
    normed = layer_norm(tokens, norm_gain, norm_bias)
    codes = row_codes(routes, gate_codes, owners, capacity)
    all_rows = lax.all_gather(normed, "exp", axis=0, tiled=True)
    all_codes = lax.all_gather(codes, "exp", axis=0, tiled=True)
    me = lax.axis_index("exp")
    weight = lax.dynamic_slice_in_dim(all_codes, me, 1, 1) * (1.0 / 1024.0)
    inner = w_out.shape[1]
    projected = jnp.dot(all_rows, w_in[0], preferred_element_type=jnp.float32)
    hidden = (jax.nn.silu(projected[:, :inner]) * projected[:, inner:]).astype(jnp.bfloat16)
    results = jnp.dot(hidden, w_out[0], preferred_element_type=jnp.float32)
    part = (results * weight).astype(jnp.bfloat16)
    return lax.psum_scatter(part, "exp", scatter_dimension=0, tiled=True)


def solution(mesh):
    return jax.shard_map(
        local,
        mesh=mesh,
        in_specs=(
            P(("seq", "exp"), None),
            P(),
            P(),
            P(("seq", "exp"), None),
            P(("seq", "exp"), None),
            P("exp", None, None),
            P("exp", None, None),
        ),
        out_specs=P(("seq", "exp"), None),
        check_vma=False,
    )
```

time: 293 us -> 151 us (0.52)
  local copies, waits for them, and re-layouts: 64.9 us -> 0.11 us
  waiting for transfers between devices: 156 us -> 96.4 us
  other arithmetic: 19.5 us -> 8.31 us
  blocking collectives: 0 us -> 10.7 us
  starting transfers between devices: 10.1 us -> 0.04 us
  matrix products: 27.7 us -> 21.4 us
    all_to_all x2 -> x0, waiting for transfers between devices: 70.9 us -> none  [the longest x1 62.3 us: local(): lax.all_to_all(results.reshape(owners, served, features), 'exp', split_ax...]
    psum x1 -> x0, waiting for transfers between devices: 68.6 us -> none  [broadcast(): return lax.psum(kept, axis)]
    reduce_scatter x0 -> x1, waiting for transfers between devices: none -> 61.9 us  [local(): return lax.psum_scatter(part, 'exp', scatter_dimension=0, tiled=True)]
    gather x2 -> x0, local copies, waits for them, and re-layouts: 21 us -> none  [the longest x1 14.3 us: local(): picked = padded_back[slot_index].reshape(count_rows, top_slots, features)]
    reshape x4 -> x0, local copies, waits for them, and re-layouts: 20.1 us -> none  [the longest x1 5.24 us: local(): received.reshape(owners * served, features)]
    all_gather x2 -> x1, waiting for transfers between devices: 15.6 us -> 34.5 us  [local(): all_rows = lax.all_gather(normed, 'exp', axis=0, tiled=True)]
    all_gather x0 -> x1, blocking collectives: none -> 10.7 us  [local(): all_codes = lax.all_gather(codes, 'exp', axis=0, tiled=True)]
    all_to_all x2 -> x0, starting transfers between devices: 9.8 us -> none  [the longest x1 5.12 us: local(): lax.all_to_all(outgoing, 'exp', split_axis=0, concat_axis=0, tiled=True)]
  transfers between devices with their start and end apart: 5 -> 2, of which waited for: 4 -> 2; matrix products, arithmetic and copies ran while one was open for 34% -> 2% of each run, Pallas kernels for 0% -> 0%
where the time goes in v1:
time: 151 us; the launch traced here: 150 us
  waiting for transfers between devices  96.4 us (64%)
  matrix products  21.4 us (14%)
  between operations  13.4 us (9%)
  blocking collectives  10.7 us (7%)
  other arithmetic  8.31 us (6%)
    reduce_scatter x1, waiting for transfers between devices, local(): return lax.psum_scatter(part, 'exp', scatter_dimension=0, tiled=True)  61.9 us
    all_gather x1, waiting for transfers between devices, local(): all_rows = lax.all_gather(normed, 'exp', axis=0, tiled=True)  34.5 us
    dot_general x1, matrix products, local(): projected = jnp.dot(all_rows, w_in[0], preferred_element_type=jnp.float32)  13.9 us
    all_gather x1, blocking collectives, local(): all_codes = lax.all_gather(codes, 'exp', axis=0, tiled=True)  10.7 us
    dot_general x1, matrix products, local(): results = jnp.dot(hidden, w_out[0], preferred_element_type=jnp.float32)  7.33 us
  transfers between devices with their start and end apart: 2, of which 2 were waited for; matrix products, arithmetic and copies ran while one was open for 2% of the time, Pallas kernels for 0%

profile of v1, /device:TPU:0, one launch (start us, length us, event | category | flops | bytes accessed | tf_op | source)
XLA Modules:
  0.0 150.4 jit_solution(2939442451663489003)
XLA Ops:
  6.5 0.0 copy-start
  6.5 0.0 all-gather.3.cloned.1.call-start
  6.5 1.5 convert_reduce_fusion
  8.0 1.5 fusion.8
  9.5 2.4 %fusion.11 = bf16[192,2048]{1,0:T(8,128)(2,1)} fusion(bf16[192,2048]{1,0:T(8,128)(2,1)} %param.7, f32[2048]{0:T(1024)} %param.9, f32[2048]{0:T(1024)} %param.8, f32[192]{0:T(256)S(1)} %add_rsqrt_fusion, f32[192]{0:T(256)S(1)} %broadcast_multiply_fusion), kind=kLoop, calls=%fused_computation.14 | loop fusion | flops 2359296 | bytes 1590784 | tf_op jit(solution)/shard_map/convert_element_type | solution.py:12
  11.9 0.0 all-gather.3.cloned.1.call-update
  12.0 0.0 reduce-scatter.2.cloned.1.call-start
  12.0 0.7 fusion.15
  12.7 0.1 convert_reduce_fusion.1
  12.9 0.7 iota_reduce_fusion
  13.5 0.6 iota_compare_fusion.3
  14.2 0.7 select_reduce_fusion
  14.9 0.1 fusion.14
  15.1 10.7 %all-gather = f32[8,192,8]{1,2,0:T(8,128)S(1)} all-gather(f32[1,192,8]{1,2,0:T(8,128)S(1)} %fusion.14), channel_id=1, replica_groups=mesh['seq'=4,'exp'=8] {'exp'}, dimensions={0}, use_global_device_ids=true | all-gather | bytes 55296 | tf_op jit(solution)/shard_map/all_gather | solution.py:37
  25.8 0.1 reshape.22
  25.9 34.5 %all-gather.3.cloned.1.call-done = bf16[1536,2048]{1,0:T(8,128)(2,1)} async-done(((bf16[192,2048]{1,0:T(8,128)(2,1)}), bf16[1536,2048]{1,0:T(8,128)(2,1)}) %all-gather.3.cloned.1.call-update) | async-done | bytes 6291472 | tf_op jit(solution)/shard_map/all_gather | solution.py:36
  60.3 13.9 %fusion = f32[1536,1408]{0,1:T(8,128)S(1)} fusion(bf16[1536,2048]{1,0:T(8,128)(2,1)} %all-gather.3.cloned.1.call-done, bf16[1,2048,1408]{2,1,0:T(8,128)(2,1)} %param.12), kind=kOutput, calls=%fused_computation.1 | convolution fusion | flops 8858370048 | bytes 20709376 | tf_op jit(solution)/shard_map/dot_general | solution.py:41
  74.3 0.0 copy-done
  74.3 7.3 %multiply_convert_fusion = bf16[1536,2048]{1,0:T(8,128)(2,1)} fusion(f32[1536]{0:T(1024)S(1)} %multiply_reduce_fusion, bf16[1,704,2048]{2,1,0:T(8,128)(2,1)S(1)} %copy-done, f32[1536,1408]{0,1:T(8,128)S(1)} %fusion), kind=kOutput, calls=%fused_computation | convolution fusion | flops 4441964544 | bytes 17831936 | tf_op jit(solution)/shard_map/dot_general | solution.py:43
  81.6 0.0 reduce-scatter.2.cloned.1.call-update
  81.7 61.9 %reduce-scatter.2.cloned.1.call-done = bf16[192,2048]{1,0:T(8,128)(2,1)} async-done(((bf16[1536,2048]{1,0:T(8,128)(2,1)}), bf16[192,2048]{1,0:T(8,128)(2,1)}) %reduce-scatter.2.cloned.1.call-update) | async-done | bytes 786448 | tf_op jit(solution)/shard_map/reduce_scatter | solution.py:45
  (4 shorter events, 0.1 us)
Async XLA Ops:
  6.5 67.8 %copy-start = (bf16[1,704,2048]{2,1,0:T(8,128)(2,1)S(1)}, bf16[1,704,2048]{2,1,0:T(8,128)(2,1)}, u32[]{:S(2)}) copy-start(bf16[1,704,2048]{2,1,0:T(8,128)(2,1)} %param.13) | copy-start | bytes 8650756
  6.5 53.8 %all-gather.3.cloned.1.call-start = ((), (), s32[]{:S(2)}) async-start(), calls=%async_computation.1 | async-start | bytes 7077888 | tf_op jit(solution)/shard_map/all_gather | solution.py:36
  12.0 131.6 %reduce-scatter.2.cloned.1.call-start = ((), (), s32[]{:S(2)}) async-start(), calls=%async_computation.2 | async-start | bytes 7077888 | tf_op jit(solution)/shard_map/reduce_scatter | solution.py:45
Sparse Core Ops, SparseCore 0:
  12.1 48.2 all-gather.2
  81.8 61.7 reduce-scatter.1

commit v2 on v1

--- a/solution.py
+++ b/solution.py
@@ -1,6 +1,8 @@
 import jax
 import jax.numpy as jnp
 from jax import lax
+from jax.experimental import pallas as pl
+from jax.experimental.pallas import tpu as pltpu
 from jax.sharding import PartitionSpec as P
 
 
@@ -27,10 +29,292 @@
     return jnp.where(kept, codes, 0.0)
 
 
+LANES = 128
+STEP = 16
+
+
+def fused(
+    owners, top, capacity, tokens, gain, bias, routes, gates, w_in_hbm, w_out_hbm, out,
+    rows_all, codes, part, sib, from_x, from_y, diag_in, proj, hid, weight, w_in, w_out,
+    load_sem, send_sem, recv_sem,
+):
+    n = tokens.shape[0]
+    half = n // 2
+    width = tokens.shape[1]
+    inner = w_out.shape[0]
+    me = lax.axis_index("exp")
+    core, across, along = me % 2, me // 2 % 2, me // 4
+
+    def peer(rel):
+        c = 1 - core if rel % 2 else core
+        x = 1 - across if rel // 2 % 2 else across
+        y = 1 - along if rel // 4 else along
+        return {"exp": y * 4 + x * 2 + c}
+
+    sibling, x_near, y_near = 1, 2, 4
+
+    def move(index, src, dst, rel):
+        return pltpu.make_async_remote_copy(
+            src_ref=src,
+            dst_ref=dst,
+            send_sem=send_sem.at[index],
+            recv_sem=recv_sem.at[index],
+            device_id=peer(rel),
+            device_id_type=pl.DeviceIdType.MESH,
+        )
+
+    first, second = pl.ds(0, n), pl.ds(n, n)
+    upper, lower = pl.ds(0, half), pl.ds(half, half)
+    load_in = pltpu.make_async_copy(w_in_hbm.at[0], w_in, load_sem.at[0])
+    load_out = pltpu.make_async_copy(w_out_hbm.at[0], w_out, load_sem.at[1])
+    load_in.start()
+    load_out.start()
+    barrier = pltpu.get_barrier_semaphore()
+    for rel in range(1, 8):
+        pl.semaphore_signal(
+            barrier, inc=1, device_id=peer(rel), device_id_type=pl.DeviceIdType.MESH
+        )
+
+    @pl.loop(0, n // STEP)
+    def _(i):
+        at = pl.ds(pl.multiple_of(i * STEP, STEP), STEP)
+        values = tokens[at, :].astype(jnp.float32)
+        average = jnp.mean(values, axis=1, keepdims=True)
+        centered = values - average
+        variance = jnp.mean(centered * centered, axis=1, keepdims=True)
+        scaled = centered * lax.rsqrt(variance + 1e-05) * gain[...] + bias[...]
+        rows_all[0, at, :] = scaled.astype(jnp.bfloat16)
+
+    pl.semaphore_wait(barrier, 7)
+    to_x = move(0, rows_all.at[0, first], rows_all.at[1, first], x_near)
+    to_y = move(1, rows_all.at[0, first], rows_all.at[2, first], y_near)
+    to_sib = move(2, rows_all.at[0, first], rows_all.at[0, second], sibling)
+    to_sib.start()
+    to_x.start()
+    to_y.start()
+
+    lane = lax.broadcasted_iota(jnp.int32, (n, LANES), 1)
+    code = jnp.zeros((n, LANES), jnp.int32)
+    named = jnp.zeros((n, LANES), jnp.float32)
+    for j in range(top):
+        match = routes[:, j : j + 1] == lane
+        code = code + jnp.where(match, gates[:, j : j + 1], 0)
+        named = named + jnp.where(match, 1.0, 0.0)
+    before = jnp.where(
+        lax.broadcasted_iota(jnp.int32, (n, n), 1) < lax.broadcasted_iota(jnp.int32, (n, n), 0),
+        1.0,
+        0.0,
+    ).astype(jnp.bfloat16)
+    rank = jnp.dot(before, named.astype(jnp.bfloat16), preferred_element_type=jnp.float32)
+    counts = jnp.sum(named, axis=0, keepdims=True)
+    most = jnp.max(counts, axis=1, keepdims=True)
+    lane_row = lane[0:1, :].astype(jnp.float32)
+    hot = jnp.min(jnp.where(counts == most, lane_row, 1e9), axis=1, keepdims=True)
+    keep = jnp.where(lane_row == hot, 1e9, float(capacity))
+    code = jnp.where(rank < keep, code, 0)
+    low = code % 4
+    high = code - low
+    row16 = lax.broadcasted_iota(jnp.int32, (2 * owners, LANES), 0)
+    lane16 = lax.broadcasted_iota(jnp.int32, (2 * owners, LANES), 1)
+
+    def turned(pick, value):
+        return lax.dot_general(
+            jnp.where(pick, 1.0, 0.0).astype(jnp.bfloat16),
+            value.astype(jnp.float32).astype(jnp.bfloat16),
+            (((1,), (1,)), ((), ())),
+            preferred_element_type=jnp.float32,
+        )
+
+    both = turned(row16 == lane16, high) + turned(row16 == lane16 + owners, low)
+    codes[0] = jnp.zeros(codes.shape[1:], jnp.bfloat16)
+    codes[0, :, 0:n] = both.astype(jnp.bfloat16)
+    code_moves = [None] + [move(7 + rel, codes.at[0], codes.at[rel], rel) for rel in range(1, 8)]
+    for rel in range(1, 8):
+        code_moves[rel].start()
+
+    choose = jnp.where((row16 == me) | (row16 == me + owners), 1.0, 0.0).astype(jnp.bfloat16)
+
+    def expert(k):
+        for c in range(2):
+            column = lax.dot_general(
+                codes[2 * k + c],
+                choose,
+                (((0,), (0,)), ((), ())),
+                preferred_element_type=jnp.float32,
+            )
+            weight[c * n : (c + 1) * n, :] = column[0:n, :] * (1.0 / 1024.0)
+
+        full = 2 * inner // 256
+
+        @pl.loop(0, full)
+        def _(i):
+            at = pl.ds(pl.multiple_of(i * 256, 256), 256)
+            proj[:, at] = jnp.dot(
+                rows_all[k], w_in[:, at], preferred_element_type=jnp.float32
+            )
+
+        if full * 256 < 2 * inner:
+            rest = pl.ds(full * 256, 2 * inner - full * 256)
+            proj[:, rest] = jnp.dot(
+                rows_all[k], w_in[:, rest], preferred_element_type=jnp.float32
+            )
+
+        wide = -(-inner // LANES) * LANES
+
+        @pl.loop(0, 2 * n // STEP)
+        def _(i):
+            at = pl.ds(pl.multiple_of(i * STEP, STEP), STEP)
+            a = proj[at, :]
+            b = pltpu.roll(a, inner, 1)[:, :wide]
+            a = a[:, :wide]
+            hid[at, :] = (a / (1.0 + jnp.exp(-a)) * b)[:, :inner].astype(jnp.bfloat16)
+
+        @pl.loop(0, width // 256)
+        def _(i):
+            at = pl.ds(pl.multiple_of(i * 256, 256), 256)
+            y = jnp.dot(hid[...], w_out[:, at], preferred_element_type=jnp.float32)
+            scale = weight[...]
+            part[k, :, at] = (y * jnp.concatenate([scale, scale], axis=1)).astype(jnp.bfloat16)
+
+    def add(dst, terms, count):
+        @pl.loop(0, count // STEP)
+        def _(i):
+            at = pl.ds(pl.multiple_of(i * STEP, STEP), STEP)
+            total = terms[0][at, :].astype(jnp.float32)
+            for term in terms[1:]:
+                total = total + term[at, :].astype(jnp.float32)
+            dst[at, :] = total.astype(jnp.bfloat16)
+
+    part_moves = [move(15 + k, part.at[k, second], sib.at[k], sibling) for k in range(4)]
+    x_sib = move(3, rows_all.at[1, first], rows_all.at[1, second], sibling)
+    y_sib = move(4, rows_all.at[2, first], rows_all.at[2, second], sibling)
+    x_on = move(5, rows_all.at[1, upper], rows_all.at[3, upper], y_near)
+    y_on = move(6, rows_all.at[2, lower], rows_all.at[3, lower], x_near)
+    d_sib = move(7, rows_all.at[3, first], rows_all.at[3, second], sibling)
+    x_up = move(19, part.at[1, upper], from_x.at[upper], x_near)
+    y_low = move(20, part.at[2, lower], from_y.at[lower], y_near)
+    d_up = move(21, part.at[3, upper], diag_in.at[upper], x_near)
+    d_low = move(22, part.at[3, lower], diag_in.at[lower], y_near)
+    x_low = move(23, part.at[1, lower], from_x.at[lower], x_near)
+    y_up = move(24, part.at[2, upper], from_y.at[upper], y_near)
+
+    def chip_sum(k):
+        part_moves[k].wait_recv()
+        mine = part.at[k, first]
+        add(mine, [mine, sib.at[k]], n)
+
+    load_in.wait()
+    load_out.wait()
+    to_sib.wait_recv()
+    code_moves[1].wait_recv()
+    expert(0)
+    part_moves[0].start()
+    to_x.wait_recv()
+    x_sib.start()
+    x_on.start()
+    to_y.wait_recv()
+    y_sib.start()
+    y_on.start()
+    code_moves[2].wait_recv()
+    code_moves[3].wait_recv()
+    x_sib.wait_recv()
+    expert(1)
+    part_moves[1].start()
+    y_sib.wait_recv()
+    code_moves[4].wait_recv()
+    code_moves[5].wait_recv()
+    chip_sum(1)
+    x_up.start()
+    expert(2)
+    part_moves[2].start()
+    x_on.wait_recv()
+    y_on.wait_recv()
+    d_sib.start()
+    code_moves[6].wait_recv()
+    code_moves[7].wait_recv()
+    chip_sum(2)
+    y_low.start()
+    d_sib.wait_recv()
+    expert(3)
+    part_moves[3].start()
+    chip_sum(3)
+    d_up.start()
+    d_low.start()
+    chip_sum(0)
+    d_up.wait_recv()
+    theirs = part.at[2, upper]
+    add(theirs, [theirs, diag_in.at[upper]], half)
+    y_up.start()
+    d_low.wait_recv()
+    theirs = part.at[1, lower]
+    add(theirs, [theirs, diag_in.at[lower]], half)
+    x_low.start()
+    x_up.wait_recv()
+    y_low.wait_recv()
+    y_up.wait_recv()
+    x_low.wait_recv()
+    add(out, [part.at[0, first], from_x, from_y], n)
+    for sent in (
+        [to_x, to_y, to_sib, x_sib, y_sib, x_on, y_on, d_sib]
+        + code_moves[1:]
+        + part_moves
+        + [x_up, y_low, d_up, d_low, x_low, y_up]
+    ):
+        sent.wait_send()
+
+
+def fused_call(tokens, norm_gain, norm_bias, routes, gate_codes, w_in, w_out, capacity):
+    owners = lax.axis_size("exp")
+    n, width = tokens.shape
+    inner = w_out.shape[1]
+    top = routes.shape[1]
+    vmem = pl.BlockSpec(memory_space=pltpu.VMEM)
+    anywhere = pl.BlockSpec(memory_space=pl.ANY)
+    bf16, f32 = jnp.bfloat16, jnp.float32
+
+    def body(*refs):
+        fused(owners, top, capacity, *refs)
+
+    flops = 2 * owners * n * width * inner * 3
+    return pl.pallas_call(
+        body,
+        out_shape=jax.ShapeDtypeStruct((n, width), bf16),
+        in_specs=[vmem] * 5 + [anywhere] * 2,
+        out_specs=vmem,
+        scratch_shapes=[
+            pltpu.VMEM((4, 2 * n, width), bf16),
+            pltpu.VMEM((8, 2 * owners, -(-n // LANES) * LANES), bf16),
+            pltpu.VMEM((4, 2 * n, width), bf16),
+            pltpu.VMEM((4, n, width), bf16),
+            pltpu.VMEM((n, width), bf16),
+            pltpu.VMEM((n, width), bf16),
+            pltpu.VMEM((n, width), bf16),
+            pltpu.VMEM((2 * n, 2 * inner), f32),
+            pltpu.VMEM((2 * n, inner), bf16),
+            pltpu.VMEM((2 * n, LANES), f32),
+            pltpu.VMEM((width, 2 * inner), bf16),
+            pltpu.VMEM((inner, width), bf16),
+            pltpu.SemaphoreType.DMA((2,)),
+            pltpu.SemaphoreType.DMA((25,)),
+            pltpu.SemaphoreType.DMA((25,)),
+        ],
+        compiler_params=pltpu.CompilerParams(
+            collective_id=0, has_side_effects=True, vmem_limit_bytes=56 * 2**20
+        ),
+        cost_estimate=pl.CostEstimate(
+            flops=flops, bytes_accessed=6 * width * inner, transcendentals=owners * n * inner
+        ),
+    )(tokens, norm_gain[None, :], norm_bias[None, :], routes, gate_codes, w_in, w_out)
+
+
 def local(tokens, norm_gain, norm_bias, routes, gate_codes, w_in, w_out):
     owners = lax.axis_size("exp")
     rows = tokens.shape[0]
     capacity = min(rows, rows * routes.shape[1] * 9 // (8 * owners))
+    if owners == 8:
+        return fused_call(
+            tokens, norm_gain, norm_bias, routes, gate_codes, w_in, w_out, capacity
+        )
     normed = layer_norm(tokens, norm_gain, norm_bias)
     codes = row_codes(routes, gate_codes, owners, capacity)
     all_rows = lax.all_gather(normed, "exp", axis=0, tiled=True)

time: 151 us -> 84.8 us (0.56)
  waiting for transfers between devices: 96.4 us -> 0 us
  Pallas kernels: 0 us -> 79.6 us
  matrix products: 21.4 us -> 0 us
  between operations: 13.4 us -> 0.01 us
  blocking collectives: 10.7 us -> 0 us
  other arithmetic: 8.31 us -> 0 us
  local copies, waits for them, and re-layouts: 0.11 us -> 5 us
    pallas_call x0 -> x1, Pallas kernels: none -> 79.6 us  [fused_call(): pl.pallas_call(body, out_shape=jax.ShapeDtypeStruct((n, width), bf16), in...]
    reduce_scatter x1 -> x0, waiting for transfers between devices: 61.9 us -> none  [local(): return lax.psum_scatter(part, 'exp', scatter_dimension=0, tiled=True)]
    all_gather x1 -> x0, waiting for transfers between devices: 34.5 us -> none  [local(): all_rows = lax.all_gather(normed, 'exp', axis=0, tiled=True)]
    dot_general x3 -> x0, matrix products: 21.4 us -> none  [the longest x1 13.9 us: local(): projected = jnp.dot(all_rows, w_in[0], preferred_element_type=jnp.float32)]
    all_gather x1 -> x0, blocking collectives: 10.7 us -> none  [local(): all_codes = lax.all_gather(codes, 'exp', axis=0, tiled=True)]
    unnamed x3, local copies, waits for them, and re-layouts: 0.09 us -> 5 us
    reduce_sum x4 -> x0, other arithmetic: 3.8 us -> none  [the longest x1 1.48 us: layer_norm(): variance = jnp.mean(centered * centered, axis=1, keepdims=True)]
    convert_element_type x1 -> x0, other arithmetic: 2.44 us -> none  [layer_norm(): (centered * lax.rsqrt(variance + 1e-05) * norm_gain + norm_bias).astype(j...]
  transfers between devices with their start and end apart: 2 -> 0, of which waited for: 2 -> 0; matrix products, arithmetic and copies ran while one was open for 2% -> 0% of each run, Pallas kernels for 0% -> 0%
where the time goes in v2:
time: 84.8 us; the launch traced here: 84.6 us
  Pallas kernels  79.6 us (94%)
  local copies, waits for them, and re-layouts  5 us (6%)
    pallas_call x1, Pallas kernels, fused_call(): pl.pallas_call(body, out_shape=jax.ShapeDtypeStruct((n, width), bf16), in...  79.6 us
    unnamed x3, local copies, waits for them, and re-layouts  5 us

profile of v2, /device:TPU:0, one launch (start us, length us, event | category | flops | bytes accessed | tf_op | source)
XLA Modules:
  0.0 84.6 jit_solution(17312150570390230581)
XLA Ops:
  0.0 1.5 %copy.8.refs_3_ = s32[192,6]{1,0:T(8,128)} copy(s32[192,6]{0,1:T(8,128)} %param.10) | data formatting | bytes 9216 | tf_op args[3]
  1.5 1.5 %copy.9.refs_4_ = s32[192,6]{1,0:T(8,128)} copy(s32[192,6]{0,1:T(8,128)} %param.11) | data formatting | bytes 9216 | tf_op args[4]
  2.9 79.6 %shard_map.73 = bf16[192,2048]{1,0:T(8,128)(2,1)} custom-call(bf16[192,2048]{1,0:T(8,128)(2,1)} %refs_0_.1, f32[1,2048]{1,0:T(1,128)} %bitcast.2, f32[1,2048]{1,0:T(1,128)} %bitcast.3, s32[192,6]{1,0:T(8,128)} %copy.8.refs_3_, s32[192,6]{1,0:T(8,128)} %copy.9.refs_4_, bf16[1,2048,1408]{2,1,0:T(8,128)(2,1)} %refs_5_.1, bf16[1,704,2048]{2,1,0:T(8,128)(2,1)} %refs_6_.1), custom_call_target="tpu_custom_call" | custom-call | flops 13287555072 | bytes 8650752 | tf_op jit(solution)/shard_map/pallas_call | solution.py:279
  82.5 2.1 %copy.11 = bf16[192,2048]{1,0:T(8,128)(2,1)} copy(bf16[192,2048]{1,0:T(8,128)(2,1)} %shard_map.73) | data formatting | bytes 1572864

commit v3 on v2

v3 whole, which is shorter than its diff:
```python
import jax
import jax.numpy as jnp
from jax import lax
from jax.experimental import pallas as pl
from jax.experimental.pallas import tpu as pltpu
from jax.sharding import PartitionSpec as P


def layer_norm(tokens, norm_gain, norm_bias):
    values = tokens.astype(jnp.float32)
    average = jnp.mean(values, axis=1, keepdims=True)
    centered = values - average
    variance = jnp.mean(centered * centered, axis=1, keepdims=True)
    return (centered * lax.rsqrt(variance + 1e-05) * norm_gain + norm_bias).astype(jnp.bfloat16)


def row_codes(routes, gate_codes, owners, capacity):
    rows = routes.shape[0]
    match = routes[:, :, None] == jnp.arange(owners, dtype=jnp.int32)[None, None, :]
    codes = jnp.sum(jnp.where(match, gate_codes[:, :, None], 0), axis=1).astype(jnp.float32)
    named = jnp.any(match, axis=1)
    before = lax.broadcasted_iota(jnp.int32, (rows, rows), 1) < lax.broadcasted_iota(
        jnp.int32, (rows, rows), 0
    )
    named_b = named.astype(jnp.bfloat16)
    rank = jnp.dot(before.astype(jnp.bfloat16), named_b, preferred_element_type=jnp.float32)
    hot = jnp.argmax(jnp.sum(named.astype(jnp.float32), axis=0))
    kept = (rank < capacity) | (jnp.arange(owners)[None, :] == hot)
    return jnp.where(kept, codes, 0.0)


LANES = 128
STEP = 16


def fused(
    owners, top, capacity, tokens, gain, bias, routes, gates, w_in_hbm, w_out_hbm, out,
    rows_all, codes, part, sib, from_x, from_y, diag_in, hid, weight, w_in, w_up, w_out,
    load_sem, send_sem, recv_sem,
):
    n = tokens.shape[0]
    half = n // 2
    width = tokens.shape[1]
    inner = w_out.shape[0]
    me = lax.axis_index("exp")
    core, across, along = me % 2, me // 2 % 2, me // 4

    def peer(rel):
        c = 1 - core if rel % 2 else core
        x = 1 - across if rel // 2 % 2 else across
        y = 1 - along if rel // 4 else along
        return {"exp": y * 4 + x * 2 + c}

    sibling, x_near, y_near = 1, 2, 4

    def move(index, src, dst, rel):
        return pltpu.make_async_remote_copy(
            src_ref=src,
            dst_ref=dst,
            send_sem=send_sem.at[index],
            recv_sem=recv_sem.at[index],
            device_id=peer(rel),
            device_id_type=pl.DeviceIdType.MESH,
        )

    first, second = pl.ds(0, n), pl.ds(n, n)
    upper, lower = pl.ds(0, half), pl.ds(half, half)
    load_in = pltpu.make_async_copy(w_in_hbm.at[0], w_in, load_sem.at[0])
    load_out = pltpu.make_async_copy(w_out_hbm.at[0], w_out, load_sem.at[1])
    load_in.start()
    load_out.start()
    barrier = pltpu.get_barrier_semaphore()
    for rel in range(1, 8):
        pl.semaphore_signal(
            barrier, inc=1, device_id=peer(rel), device_id_type=pl.DeviceIdType.MESH
        )

    @pl.loop(0, n // STEP)
    def _(i):
        at = pl.ds(pl.multiple_of(i * STEP, STEP), STEP)
        values = tokens[at, :].astype(jnp.float32)
        average = jnp.mean(values, axis=1, keepdims=True)
        centered = values - average
        variance = jnp.mean(centered * centered, axis=1, keepdims=True)
        scaled = centered * lax.rsqrt(variance + 1e-05) * gain[...] + bias[...]
        rows_all[0, at, :] = scaled.astype(jnp.bfloat16)

    pl.semaphore_wait(barrier, 7)
    a_x = move(0, rows_all.at[0, upper], rows_all.at[1, upper], x_near)
    b_y = move(1, rows_all.at[0, lower], rows_all.at[1, lower], y_near)
    to_sib = move(2, rows_all.at[0, first], rows_all.at[0, second], sibling)
    a_x.start()
    b_y.start()
    to_sib.start()

    expert_row = lax.broadcasted_iota(jnp.int32, (owners, n), 0)
    code = jnp.zeros((owners, n), jnp.int32)
    named = jnp.zeros((owners, n), jnp.float32)
    for j in range(top):
        match = routes[j : j + 1, :] == expert_row
        code = code + jnp.where(match, gates[j : j + 1, :], 0)
        named = named + jnp.where(match, 1.0, 0.0)
    before = jnp.where(
        lax.broadcasted_iota(jnp.int32, (n, n), 0) < lax.broadcasted_iota(jnp.int32, (n, n), 1),
        1.0,
        0.0,
    ).astype(jnp.bfloat16)
    rank = jnp.dot(named.astype(jnp.bfloat16), before, preferred_element_type=jnp.float32)
    counts = jnp.sum(named, axis=1, keepdims=True)
    most = jnp.max(counts, axis=0, keepdims=True)
    index = expert_row.astype(jnp.float32)
    hot = jnp.min(jnp.where(counts == most, index, 1e9), axis=0, keepdims=True)
    code = jnp.where((rank < capacity) | (index == hot), code, 0)
    low = code % 4
    both = jnp.concatenate([code - low, low], axis=0).astype(jnp.float32)
    codes[0] = jnp.zeros(codes.shape[1:], jnp.bfloat16)
    codes[0, :, 0:n] = both.astype(jnp.bfloat16)
    code_moves = [None] + [move(7 + rel, codes.at[0], codes.at[rel], rel) for rel in range(1, 8)]
    for rel in range(1, 8):
        code_moves[rel].start()

    row16 = lax.broadcasted_iota(jnp.int32, (2 * owners, LANES), 0)
    choose = jnp.where((row16 == me) | (row16 == me + owners), 1.0, 0.0).astype(jnp.bfloat16)

    up_width = w_up.shape[1]

    def expert(k):
        if k == 0:
            pieces = ((0, 0, 0, n), (n, 1, 0, n))
        elif k == 2:
            pieces = ((0, 6, 0, n), (n, 7, 0, n))
        else:
            x_from, y_from = (0, half) if k == 1 else (half, 0)
            pieces = (
                (0, 2, x_from, half), (half, 4, y_from, half),
                (n, 3, x_from, half), (n + half, 5, y_from, half),
            )
        for at, slot, start, count in pieces:
            column = lax.dot_general(
                codes[slot],
                choose,
                (((0,), (0,)), ((), ())),
                preferred_element_type=jnp.float32,
            )
            weight[at : at + count, :] = column[start : start + count, :] * (1.0 / 1024.0)

        @pl.loop(0, up_width // 256)
        def _(i):
            at = pl.ds(pl.multiple_of(i * 256, 256), 256)
            a = jnp.dot(rows_all[k], w_in[:, at], preferred_element_type=jnp.float32)
            b = jnp.dot(rows_all[k], w_up[:, at], preferred_element_type=jnp.float32)
            hid[:, at] = (a / (1.0 + jnp.exp(-a)) * b).astype(jnp.bfloat16)

        @pl.loop(0, width // 256)
        def _(i):
            at = pl.ds(pl.multiple_of(i * 256, 256), 256)
            y = jnp.dot(hid[:, :inner], w_out[:, at], preferred_element_type=jnp.float32)
            scale = weight[...]
            part[k, :, at] = (y * jnp.concatenate([scale, scale], axis=1)).astype(jnp.bfloat16)

    def add(dst, terms, count):
        @pl.loop(0, count // STEP)
        def _(i):
            at = pl.ds(pl.multiple_of(i * STEP, STEP), STEP)
            total = terms[0][at, :].astype(jnp.float32)
            for term in terms[1:]:
                total = total + term[at, :].astype(jnp.float32)
            dst[at, :] = total.astype(jnp.bfloat16)

    part_moves = [move(3 + k, part.at[k, second], sib.at[k], sibling) for k in range(4)]
    row_sib = [None] + [
        move(14 + k, rows_all.at[k, first], rows_all.at[k, second], sibling) for k in range(1, 4)
    ]
    x_on = move(18, rows_all.at[1, upper], rows_all.at[2, upper], y_near)
    y_on = move(19, rows_all.at[1, lower], rows_all.at[2, lower], x_near)
    b_x = move(20, rows_all.at[0, lower], rows_all.at[3, upper], x_near)
    a_y = move(21, rows_all.at[0, upper], rows_all.at[3, lower], y_near)
    sum_a_x = move(22, part.at[1, upper], from_x.at[upper], x_near)
    sum_b_y = move(23, part.at[1, lower], from_y.at[lower], y_near)
    sum_d_x = move(24, part.at[2, upper], diag_in.at[upper], x_near)
    sum_d_y = move(25, part.at[2, lower], diag_in.at[lower], y_near)
    sum_b_x = move(26, part.at[3, upper], from_x.at[lower], x_near)
    sum_a_y = move(27, part.at[3, lower], from_y.at[upper], y_near)

    load_in.wait()

    @pl.loop(0, width // STEP)
    def _(i):
        at = pl.ds(pl.multiple_of(i * STEP, STEP), STEP)
        turned_in = pltpu.roll(w_in[at, :].astype(jnp.float32), inner, 1)
        w_up[at, :] = turned_in[:, :up_width].astype(jnp.bfloat16)

    load_out.wait()
    to_sib.wait_recv()
    code_moves[1].wait_recv()
    expert(0)
    part_moves[0].start()
    a_x.wait_recv()
    x_on.start()
    b_y.wait_recv()
    y_on.start()
    row_sib[1].start()
    b_x.start()
    a_y.start()
    for rel in range(2, 8):
        code_moves[rel].wait_recv()
    row_sib[1].wait_recv()
    expert(1)
    part_moves[1].start()
    part_moves[1].wait_recv()
    mine = part.at[1, first]
    add(mine, [mine, sib.at[1]], n)
    sum_a_x.start()
    sum_b_y.start()
    x_on.wait_recv()
    y_on.wait_recv()
    row_sib[2].start()
    row_sib[2].wait_recv()
    expert(2)
    part_moves[2].start()
    part_moves[2].wait_recv()
    mine = part.at[2, first]
    add(mine, [mine, sib.at[2]], n)
    sum_d_x.start()
    sum_d_y.start()
    b_x.wait_recv()
    a_y.wait_recv()
    row_sib[3].start()
    row_sib[3].wait_recv()
    expert(3)
    part_moves[3].start()
    part_moves[3].wait_recv()
    sum_d_x.wait_recv()
    mine = part.at[3, lower]
    add(mine, [mine, sib.at[3, lower], diag_in.at[upper]], half)
    sum_a_y.start()
    sum_d_y.wait_recv()
    mine = part.at[3, upper]
    add(mine, [mine, sib.at[3, upper], diag_in.at[lower]], half)
    sum_b_x.start()
    part_moves[0].wait_recv()
    sum_a_x.wait_recv()
    sum_b_y.wait_recv()
    sum_a_y.wait_recv()
    sum_b_x.wait_recv()
    add(out, [part.at[0, first], sib.at[0], from_x, from_y], n)
    for sent in (
        [a_x, b_y, to_sib, x_on, y_on, b_x, a_y]
        + row_sib[1:]
        + code_moves[1:]
        + part_moves
        + [sum_a_x, sum_b_y, sum_d_x, sum_d_y, sum_b_x, sum_a_y]
    ):
        sent.wait_send()


def fused_call(tokens, norm_gain, norm_bias, routes, gate_codes, w_in, w_out, capacity):
    owners = lax.axis_size("exp")
    n, width = tokens.shape
    inner = w_out.shape[1]
    top = routes.shape[1]
    wide = -(-inner // 256) * 256
    vmem = pl.BlockSpec(memory_space=pltpu.VMEM)
    anywhere = pl.BlockSpec(memory_space=pl.ANY)
    bf16, f32 = jnp.bfloat16, jnp.float32

    def body(*refs):
        fused(owners, top, capacity, *refs)

    flops = 2 * owners * n * width * inner * 3
    return pl.pallas_call(
        body,
        out_shape=jax.ShapeDtypeStruct((n, width), bf16),
        in_specs=[vmem] * 5 + [anywhere] * 2,
        out_specs=vmem,
        scratch_shapes=[
            pltpu.VMEM((4, 2 * n, width), bf16),
            pltpu.VMEM((8, 2 * owners, -(-n // LANES) * LANES), bf16),
            pltpu.VMEM((4, 2 * n, width), bf16),
            pltpu.VMEM((4, n, width), bf16),
            pltpu.VMEM((n, width), bf16),
            pltpu.VMEM((n, width), bf16),
            pltpu.VMEM((n, width), bf16),
            pltpu.VMEM((2 * n, wide), bf16),
            pltpu.VMEM((2 * n, LANES), f32),
            pltpu.VMEM((width, 2 * inner), bf16),
            pltpu.VMEM((width, wide), bf16),
            pltpu.VMEM((inner, width), bf16),
            pltpu.SemaphoreType.DMA((2,)),
            pltpu.SemaphoreType.DMA((28,)),
            pltpu.SemaphoreType.DMA((28,)),
        ],
        compiler_params=pltpu.CompilerParams(
            collective_id=0, has_side_effects=True, vmem_limit_bytes=56 * 2**20
        ),
        cost_estimate=pl.CostEstimate(
            flops=flops, bytes_accessed=6 * width * inner, transcendentals=owners * n * inner
        ),
    )(tokens, norm_gain[None, :], norm_bias[None, :], routes.T, gate_codes.T, w_in, w_out)


def local(tokens, norm_gain, norm_bias, routes, gate_codes, w_in, w_out):
    owners = lax.axis_size("exp")
    rows = tokens.shape[0]
    capacity = min(rows, rows * routes.shape[1] * 9 // (8 * owners))
    if owners == 8:
        return fused_call(
            tokens, norm_gain, norm_bias, routes, gate_codes, w_in, w_out, capacity
        )
    normed = layer_norm(tokens, norm_gain, norm_bias)
    codes = row_codes(routes, gate_codes, owners, capacity)
    all_rows = lax.all_gather(normed, "exp", axis=0, tiled=True)
    all_codes = lax.all_gather(codes, "exp", axis=0, tiled=True)
    me = lax.axis_index("exp")
    weight = lax.dynamic_slice_in_dim(all_codes, me, 1, 1) * (1.0 / 1024.0)
    inner = w_out.shape[1]
    projected = jnp.dot(all_rows, w_in[0], preferred_element_type=jnp.float32)
    hidden = (jax.nn.silu(projected[:, :inner]) * projected[:, inner:]).astype(jnp.bfloat16)
    results = jnp.dot(hidden, w_out[0], preferred_element_type=jnp.float32)
    part = (results * weight).astype(jnp.bfloat16)
    return lax.psum_scatter(part, "exp", scatter_dimension=0, tiled=True)


def solution(mesh):
    return jax.shard_map(
        local,
        mesh=mesh,
        in_specs=(
            P(("seq", "exp"), None),
            P(),
            P(),
            P(("seq", "exp"), None),
            P(("seq", "exp"), None),
            P("exp", None, None),
            P("exp", None, None),
        ),
        out_specs=P(("seq", "exp"), None),
        check_vma=False,
    )
```

time: 84.8 us -> 71.8 us (0.85)
  Pallas kernels: 79.6 us -> 69.5 us
  local copies, waits for them, and re-layouts: 5 us -> 2.09 us
    pallas_call x1, Pallas kernels: 79.6 us -> 69.5 us  [fused_call(): pl.pallas_call(body, out_shape=jax.ShapeDtypeStruct((n, width), bf16), in...]
    unnamed x3 -> x1, local copies, waits for them, and re-layouts: 5 us -> 2.09 us
where the time goes in v3:
time: 71.8 us; the launch traced here: 71.6 us
  Pallas kernels  69.5 us (97%)
  local copies, waits for them, and re-layouts  2.09 us (3%)
    pallas_call x1, Pallas kernels, fused_call(): pl.pallas_call(body, out_shape=jax.ShapeDtypeStruct((n, width), bf16), in...  69.5 us
    unnamed x1, local copies, waits for them, and re-layouts  2.09 us

profile of v3, /device:TPU:0, one launch (start us, length us, event | category | flops | bytes accessed | tf_op | source)
XLA Modules:
  0.0 71.6 jit_solution(2086399742335508634)
XLA Ops:
  0.0 69.5 %shard_map.73 = bf16[192,2048]{1,0:T(8,128)(2,1)} custom-call(bf16[192,2048]{1,0:T(8,128)(2,1)} %refs_0_.1, f32[1,2048]{1,0:T(1,128)} %bitcast.4, f32[1,2048]{1,0:T(1,128)} %bitcast.5, s32[6,192]{1,0:T(8,128)} %bitcast.6, s32[6,192]{1,0:T(8,128)} %bitcast.7, bf16[1,2048,1408]{2,1,0:T(8,128)(2,1)} %refs_5_.1, bf16[1,704,2048]{2,1,0:T(8,128)(2,1)} %refs_6_.1), custom_call_target="tpu_custom_call" | custom-call | flops 13287555072 | bytes 8650752 | tf_op jit(solution)/shard_map/pallas_call | solution.py:271
  69.5 2.1 %copy.9 = bf16[192,2048]{1,0:T(8,128)(2,1)} copy(bf16[192,2048]{1,0:T(8,128)(2,1)} %shard_map.73) | data formatting | bytes 1572864

commit v4 on v3

--- a/solution.py
+++ b/solution.py
@@ -34,8 +34,8 @@
 
 
 def fused(
-    owners, top, capacity, tokens, gain, bias, routes, gates, w_in_hbm, w_out_hbm, out,
-    rows_all, codes, part, sib, from_x, from_y, diag_in, hid, weight, w_in, w_up, w_out,
+    owners, top, capacity, tokens, gain, bias, routes, gates, w_in_hbm, w_out_hbm, base_out, from_x, from_y,
+    rows_all, codes, part, sib, diag_in, base, hid, weight, w_in, w_up, w_out,
     load_sem, send_sem, recv_sem,
 ):
     n = tokens.shape[0]
@@ -165,7 +165,7 @@
             total = terms[0][at, :].astype(jnp.float32)
             for term in terms[1:]:
                 total = total + term[at, :].astype(jnp.float32)
-            dst[at, :] = total.astype(jnp.bfloat16)
+            dst[at, :] = total.astype(dst.dtype)
 
     part_moves = [move(3 + k, part.at[k, second], sib.at[k], sibling) for k in range(4)]
     row_sib = [None] + [
@@ -182,6 +182,9 @@
     sum_b_x = move(26, part.at[3, upper], from_x.at[lower], x_near)
     sum_a_y = move(27, part.at[3, lower], from_y.at[upper], y_near)
 
+    b_x.start()
+    a_y.start()
+
     load_in.wait()
 
     @pl.loop(0, width // STEP)
@@ -200,10 +203,12 @@
     b_y.wait_recv()
     y_on.start()
     row_sib[1].start()
-    b_x.start()
-    a_y.start()
     for rel in range(2, 8):
         code_moves[rel].wait_recv()
+    part_moves[0].wait_recv()
+    add(base, [part.at[0, first], sib.at[0]], n)
+    base_move = pltpu.make_async_copy(base, base_out, load_sem.at[2])
+    base_move.start()
     row_sib[1].wait_recv()
     expert(1)
     part_moves[1].start()
@@ -238,12 +243,11 @@
     mine = part.at[3, upper]
     add(mine, [mine, sib.at[3, upper], diag_in.at[lower]], half)
     sum_b_x.start()
-    part_moves[0].wait_recv()
     sum_a_x.wait_recv()
     sum_b_y.wait_recv()
     sum_a_y.wait_recv()
     sum_b_x.wait_recv()
-    add(out, [part.at[0, first], sib.at[0], from_x, from_y], n)
+    base_move.wait()
     for sent in (
         [a_x, b_y, to_sib, x_on, y_on, b_x, a_y]
         + row_sib[1:]
@@ -268,25 +272,24 @@
         fused(owners, top, capacity, *refs)
 
     flops = 2 * owners * n * width * inner * 3
-    return pl.pallas_call(
+    base, from_x, from_y = pl.pallas_call(
         body,
-        out_shape=jax.ShapeDtypeStruct((n, width), bf16),
+        out_shape=[jax.ShapeDtypeStruct((n, width), kind) for kind in (f32, bf16, bf16)],
         in_specs=[vmem] * 5 + [anywhere] * 2,
-        out_specs=vmem,
+        out_specs=[anywhere] * 3,
         scratch_shapes=[
             pltpu.VMEM((4, 2 * n, width), bf16),
             pltpu.VMEM((8, 2 * owners, -(-n // LANES) * LANES), bf16),
             pltpu.VMEM((4, 2 * n, width), bf16),
             pltpu.VMEM((4, n, width), bf16),
             pltpu.VMEM((n, width), bf16),
-            pltpu.VMEM((n, width), bf16),
-            pltpu.VMEM((n, width), bf16),
+            pltpu.VMEM((n, width), f32),
             pltpu.VMEM((2 * n, wide), bf16),
             pltpu.VMEM((2 * n, LANES), f32),
             pltpu.VMEM((width, 2 * inner), bf16),
             pltpu.VMEM((width, wide), bf16),
             pltpu.VMEM((inner, width), bf16),
-            pltpu.SemaphoreType.DMA((2,)),
+            pltpu.SemaphoreType.DMA((3,)),
             pltpu.SemaphoreType.DMA((28,)),
             pltpu.SemaphoreType.DMA((28,)),
         ],
@@ -297,6 +300,7 @@
             flops=flops, bytes_accessed=6 * width * inner, transcendentals=owners * n * inner
         ),
     )(tokens, norm_gain[None, :], norm_bias[None, :], routes.T, gate_codes.T, w_in, w_out)
+    return (base + from_x.astype(f32) + from_y.astype(f32)).astype(bf16)
 
 
 def local(tokens, norm_gain, norm_bias, routes, gate_codes, w_in, w_out):

time: 71.8 us -> 68 us (0.947)
  Pallas kernels: 69.5 us -> 64.8 us
  other arithmetic: 0 us -> 3.05 us
  local copies, waits for them, and re-layouts: 2.09 us -> 0 us
    pallas_call x1, Pallas kernels: 69.5 us -> 64.8 us  [fused_call(): pl.pallas_call(body, out_shape=[jax.ShapeDtypeStruct((n, width), kind) fo...]
    convert_element_type x0 -> x1, other arithmetic: none -> 3.05 us  [fused_call(): return (base + from_x.astype(f32) + from_y.astype(f32)).astype(bf16)]
    unnamed x1 -> x0, local copies, waits for them, and re-layouts: 2.09 us -> none
where the time goes in v4:
time: 68 us; the launch traced here: 67.8 us
  Pallas kernels  64.8 us (95%)
  other arithmetic  3.05 us (4%)
    pallas_call x1, Pallas kernels, fused_call(): pl.pallas_call(body, out_shape=[jax.ShapeDtypeStruct((n, width), kind) fo...  64.8 us
    convert_element_type x1, other arithmetic, fused_call(): return (base + from_x.astype(f32) + from_y.astype(f32)).astype(bf16)  3.05 us

profile of v4, /device:TPU:0, one launch (start us, length us, event | category | flops | bytes accessed | tf_op | source)
XLA Modules:
  0.0 67.8 jit_solution(9701360077115128343)
XLA Ops:
  0.0 64.8 %shard_map.73 = (f32[192,2048]{1,0:T(8,128)}, bf16[192,2048]{1,0:T(8,128)(2,1)}, bf16[192,2048]{1,0:T(8,128)(2,1)}) custom-call(bf16[192,2048]{1,0:T(8,128)(2,1)} %refs_0_.1, f32[1,2048]{1,0:T(1,128)} %bitcast.4, f32[1,2048]{1,0:T(1,128)} %bitcast.5, s32[6,192]{1,0:T(8,128)} %bitcast.6, s32[6,192]{1,0:T(8,128)} %bitcast.7, bf16[1,2048,1408]{2,1,0:T(8,128)(2,1)} %refs_5_.1, ...), custom_call_target="tpu_custom_call" | custom-call | flops 13287555072 | bytes 8650752 | tf_op jit(solution)/shard_map/pallas_call | solution.py:275
  64.8 3.0 %add_convert_fusion = bf16[192,2048]{1,0:T(8,128)(2,1)} fusion(bf16[192,2048]{1,0:T(8,128)(2,1)} %get-tuple-element.10, f32[192,2048]{1,0:T(8,128)} %get-tuple-element.8, bf16[192,2048]{1,0:T(8,128)(2,1)} %get-tuple-element.9), kind=kLoop, calls=%fused_computation | loop fusion | flops 1966080 | bytes 3932160 | tf_op jit(solution)/shard_map/convert_element_type | solution.py:303
